TPU v7x, 256 devices: a whole 4x4x8 slice. The times are simulated.
256 devices in a mesh: rep: 16 (over x, z_lo, core), tp: 16 (over y, z_hi).
Axes of the slice: x: 4, y: 4, z: 8 (z_hi: 4, z_lo: 2; z = z_hi * 2 + z_lo), core: 2. Of those that a mesh axis runs over, the one named last changes fastest.
Arguments:
- acts: bfloat16 [6144, 8192], P('rep', 'tp'), may hold values from -6 to 6
- base_weight: bfloat16 [8192, 8192], P('tp'), may hold values from -0.0625 to 0.0625
- a_high: bfloat16 [32, 128, 8192], P('rep', None, 'tp'), may hold values from -0.0625 to 0.0625
- b_high: bfloat16 [32, 128, 8192], P('rep', None, 'tp'), may hold values from -0.5 to 0.5
- a_mid: bfloat16 [64, 32, 8192], P('rep', None, 'tp'), may hold values from -0.0625 to 0.0625
- b_mid: bfloat16 [64, 32, 8192], P('rep', None, 'tp'), may hold values from -1 to 1
- a_low: bfloat16 [128, 8, 8192], P('rep', None, 'tp'), may hold values from -0.0625 to 0.0625
- b_low: bfloat16 [128, 8, 8192], P('rep', None, 'tp'), may hold values from -2 to 2
- row_adapter: int32 [6144], P('rep'), may hold values from 0 to 223
- home_high: int32 [32], replicated, may hold values from 0 to 31, each once
- home_mid: int32 [64], replicated, may hold values from 0 to 63, each once
- home_low: int32 [128], replicated, may hold values from 0 to 127, each once
Outputs:
- projected: bfloat16 [6144, 8192], P('rep', 'tp')
All inputs are finite; a program needn't handle non-finite values.
Results may differ from a plain program's by a relative error of at most 0.0039.
Values may be sent and summed in bfloat16 or wider, within the bound.
A program may use at most 128 MiB of HBM per device.

v0:
```python
import jax
import jax.numpy as jnp
from jax import lax
from jax.sharding import PartitionSpec as P


def store_rows(ids, home, offset):
    local = ids - offset
    count = home.shape[0]
    match = local[:, None] == jnp.arange(count, dtype=jnp.int32)[None, :]
    return jnp.sum(jnp.where(match, home[None, :] + 1, 0), axis=1) - 1


def shrink_part(inputs, piece, rows_k):
    count, rank, width = piece.shape
    total = inputs.shape[0]
    products = jnp.einsum(
        "rd,kd->rk", inputs, piece.reshape(count * rank, width), preferred_element_type=jnp.float32
    )
    chosen = rows_k[:, None] == jnp.arange(count, dtype=jnp.int32)[None, :]
    return jnp.sum(products.reshape(total, count, rank) * chosen[:, :, None], axis=1)


def spread_rows(shrink, rows_k, count):
    total, rank = shrink.shape
    chosen = rows_k[:, None] == jnp.arange(count, dtype=jnp.int32)[None, :]
    spread = jnp.where(chosen[:, :, None], shrink[:, None, :], jnp.zeros((), jnp.bfloat16))
    return spread.reshape(total, count * rank)


def shards(
    acts,
    base_weight,
    a_high,
    b_high,
    a_mid,
    b_mid,
    a_low,
    b_low,
    row_adapter,
    home_high,
    home_mid,
    home_low,
):
    offsets = (0, home_high.shape[0], home_high.shape[0] + home_mid.shape[0])
    homes = (home_high, home_mid, home_low)
    width = acts.shape[1]
    rows_k = tuple((store_rows(row_adapter, homes[b], offsets[b]) for b in range(3)))
    total = acts.shape[0]
    pieces = (
        lax.all_gather(a_high, "rep", axis=0, tiled=True),
        lax.all_gather(a_mid, "rep", axis=0, tiled=True),
        lax.all_gather(a_low, "rep", axis=0, tiled=True),
    )
    partial_value = tuple((shrink_part(acts, pieces[b], rows_k[b]) for b in range(3)))
    summed = lax.psum((partial_value[0], partial_value[1], partial_value[2]), "tp")
    shrink = tuple((value.astype(jnp.bfloat16) for value in summed))
    pieces = (
        lax.all_gather(b_high, "rep", axis=0, tiled=True),
        lax.all_gather(b_mid, "rep", axis=0, tiled=True),
        lax.all_gather(b_low, "rep", axis=0, tiled=True),
    )
    result = jnp.zeros((total, width), jnp.float32)
    for b in range(3):
        count, rank, cols = pieces[b].shape
        spread = spread_rows(shrink[b], rows_k[b], count)
        result = result + jnp.dot(
            spread, pieces[b].reshape(count * rank, cols), preferred_element_type=jnp.float32
        )
    base_terms = jnp.dot(acts, base_weight, preferred_element_type=jnp.float32)
    base = lax.psum_scatter(base_terms, "tp", scatter_dimension=1, tiled=True)
    return (base + result).astype(jnp.bfloat16)


def solution(mesh):
    return jax.shard_map(
        shards,
        mesh=mesh,
        in_specs=(
            P("rep", "tp"),
            P("tp", None),
            P("rep", None, "tp"),
            P("rep", None, "tp"),
            P("rep", None, "tp"),
            P("rep", None, "tp"),
            P("rep", None, "tp"),
            P("rep", None, "tp"),
            P("rep"),
            P(),
            P(),
            P(),
        ),
        out_specs=P("rep", "tp"),
        check_vma=False,
    )
```

profile of v0, /device:TPU:1, one launch (start us, length us, event | category | flops | bytes accessed | tf_op | source)
XLA Modules:
  0.0 343.4 jit_solution(11238750943534961013)
XLA Ops:
  7.4 0.7 all-gather.15.cloned.1.call-update
  8.1 0.0 all-gather.11.cloned.1.call-start
  8.1 0.7 all-gather.11.cloned.1.call-update
  8.8 0.0 all-gather.7.cloned.1.call-start
  8.9 0.7 all-gather.7.cloned.1.call-update
  9.6 0.0 all-gather.17.cloned.1.call-start
  9.6 1.5 copy.38
  11.1 0.0 all-gather.9.cloned.1.call-start
  11.2 0.5 all-gather.9.cloned.1.call-update
  11.7 0.0 all-gather.13.cloned.1.call-start
  11.8 0.5 all-gather.13.cloned.1.call-update
  12.3 0.0 reduce-scatter.2.cloned.1.call-start
  12.4 9.7 %fusion.57 = f32[384,8192]{1,0:T(8,128)} fusion(bf16[384,512]{1,0:T(8,128)(2,1)S(1)} %copy-done, bf16[512,8192]{1,0:T(8,128)(2,1)} %param.13), kind=kOutput, calls=%fused_computation.54 | convolution fusion | flops 3221225472 | bytes 21364736 | tf_op jit(solution)/shard_map/dot_general | solution.py:70
  22.2 0.6 copy-done.2
  22.8 0.0 copy-done.1
  22.8 0.2 select_reduce_fusion
  23.1 0.2 copy.34
  23.3 0.1 select_reduce_fusion.2
  23.4 0.1 select_reduce_fusion.1
  23.6 40.2 %all-gather.15.cloned.1.call-done = bf16[128,8,512]{2,1,0:T(8,128)(2,1)} async-done(((bf16[8,8,512]{2,1,0:T(8,128)(2,1)}), bf16[128,8,512]{2,1,0:T(8,128)(2,1)}) %all-gather.15.cloned.1.call-update) | async-done | bytes 1048592 | tf_op jit(solution)/shard_map/all_gather | solution.py:53
  63.8 2.0 multiply_reduce_fusion.2
  65.8 67.6 %all-gather.11.cloned.1.call-done = bf16[64,32,512]{2,1,0:T(8,128)(2,1)} async-done(((bf16[4,32,512]{2,1,0:T(8,128)(2,1)}), bf16[64,32,512]{2,1,0:T(8,128)(2,1)}) %all-gather.11.cloned.1.call-update) | async-done | bytes 2097168 | tf_op jit(solution)/shard_map/all_gather | solution.py:52
  133.4 3.3 multiply_reduce_fusion.1
  136.7 77.2 %all-gather.7.cloned.1.call-done = bf16[32,128,512]{2,1,0:T(8,128)(2,1)} async-done(((bf16[2,128,512]{2,1,0:T(8,128)(2,1)}), bf16[32,128,512]{2,1,0:T(8,128)(2,1)}) %all-gather.7.cloned.1.call-update) | async-done | bytes 4194320 | tf_op jit(solution)/shard_map/all_gather | solution.py:51
  213.9 3.7 %multiply_reduce_fusion = f32[384,128]{1,0:T(8,128)S(1)} fusion(f32[384,32]{0,1:T(8,128)S(1)} %get-tuple-element.11, bf16[32,128,512]{2,1,0:T(8,128)(2,1)} %all-gather.7.cloned.1.call-done, bf16[384,512]{1,0:T(8,128)(2,1)S(1)} %copy-done), kind=kOutput, calls=%fused_computation | convolution fusion | flops 1613709312 | bytes 4833280 | tf_op jit(solution)/shard_map/rd,kd->rk/dot_general | solution.py:17
  217.6 71.1 %all-reduce.2 = (bf16[384,8]{0,1:T(8,128)(2,1)S(1)}, bf16[384,128]{1,0:T(8,128)(2,1)S(1)}, bf16[384,32]{0,1:T(8,128)(2,1)S(1)}) all-reduce(f32[384,8]{0,1:T(8,128)S(1)} %multiply_reduce_fusion.2, f32[384,128]{1,0:T(8,128)S(1)} %multiply_reduce_fusion, f32[384,32]{0,1:T(8,128)S(1)} %multiply_reduce_fusion.1), channel_id=1, replica_groups=mesh['rep'=16,'tp'=16] {'tp'}, use_global_device_ids=true, to_apply=%region_9.10 | all-reduce | flops 64512 | bytes 387072 | tf_op jit(solution)/shard_map/psum | solution.py:56
  288.7 0.0 all-gather.17.cloned.1.call-done
  288.7 1.8 convolution_bitcast_fusion
  290.6 2.0 all-gather.9.cloned.1.call-done
  292.5 4.1 %fusion.13 = f32[384,512]{1,0:T(8,128)S(1)} fusion(bf16[32,128,512]{2,1,0:T(8,128)(2,1)} %all-gather.9.cloned.1.call-done, pred[384,32]{0,1:T(8,128)(4,1)S(1)} %get-tuple-element.10, bf16[384,128]{1,0:T(8,128)(2,1)S(1)} %get-tuple-element.6), kind=kOutput, calls=%fused_computation.14 | convolution fusion | flops 1612185600 | bytes 5091328 | tf_op jit(solution)/shard_map/dot_general | solution.py:67
  296.6 34.0 %all-gather.13.cloned.1.call-done = bf16[64,32,512]{2,1,0:T(8,128)(2,1)} async-done(((bf16[4,32,512]{2,1,0:T(8,128)(2,1)}), bf16[64,32,512]{2,1,0:T(8,128)(2,1)}) %all-gather.13.cloned.1.call-update) | async-done | bytes 2097168 | tf_op jit(solution)/shard_map/all_gather | solution.py:60
  330.6 5.3 %fusion.36 = bf16[384,512]{1,0:T(8,128)(2,1)} fusion(f32[384,512]{1,0:T(8,128)} %reduce-scatter.2.cloned.1.call-done, f32[384,512]{1,0:T(8,128)S(1)} %convolution_bitcast_fusion, f32[384,512]{1,0:T(8,128)S(1)} %fusion.13, bf16[64,32,512]{2,1,0:T(8,128)(2,1)} %all-gather.13.cloned.1.call-done, pred[384,64]{0,1:T(8,128)(4,1)S(1)} %get-tuple-element.8, ...), kind=kOutput, calls=%fused_computation.20 | convolution fusion | flops 806879232 | bytes 4898816 | tf_op jit(solution)/shard_map/dot_general | solution.py:67
  (22 shorter events, 0.2 us)
Async XLA Ops:
  7.4 5.0 %copy-start = (bf16[384,512]{1,0:T(8,128)(2,1)S(1)}, bf16[384,512]{1,0:T(8,128)(2,1)}, u32[]{:S(2)}) copy-start(bf16[384,512]{1,0:T(8,128)(2,1)} %param.12) | copy-start | bytes 1179652
  7.4 56.4 %all-gather.15.cloned.1.call-start = ((), (), s32[]{:S(2)}) async-start(), calls=%async_computation.6 | async-start | bytes 1114112 | tf_op jit(solution)/shard_map/all_gather | solution.py:53
  8.1 125.3 %all-gather.11.cloned.1.call-start = ((), (), s32[]{:S(2)}) async-start(), calls=%async_computation.4 | async-start | bytes 2228224 | tf_op jit(solution)/shard_map/all_gather | solution.py:52
  8.8 205.1 %all-gather.7.cloned.1.call-start = ((), (), s32[]{:S(2)}) async-start(), calls=%async_computation.2 | async-start | bytes 4456448 | tf_op jit(solution)/shard_map/all_gather | solution.py:51
  9.6 279.1 %all-gather.17.cloned.1.call-start = ((), (), s32[]{:S(2)}) async-start(), calls=%async_computation.7 | async-start | bytes 1114112 | tf_op jit(solution)/shard_map/all_gather | solution.py:61
  11.1 281.4 %all-gather.9.cloned.1.call-start = ((), (), s32[]{:S(2)}) async-start(), calls=%async_computation.3 | async-start | bytes 4456448 | tf_op jit(solution)/shard_map/all_gather | solution.py:59
  11.7 318.9 %all-gather.13.cloned.1.call-start = ((), (), s32[]{:S(2)}) async-start(), calls=%async_computation.5 | async-start | bytes 2228224 | tf_op jit(solution)/shard_map/all_gather | solution.py:60
  12.3 318.3 %reduce-scatter.2.cloned.1.call-start = ((), (), s32[]{:S(2)}) async-start(), calls=%async_computation.1 | async-start | bytes 13369344 | tf_op jit(solution)/shard_map/reduce_scatter | solution.py:71
  22.1 0.7 copy-start.2
  22.1 0.7 copy-start.1
  22.1 1.2 copy-start.3
  22.1 1.3 copy-start.4
Sparse Core Ops, SparseCore 0:
  10.0 53.6 all-gather.14
  65.6 67.7 all-gather.10
  135.3 78.6 all-gather.6
  215.6 34.0 all-gather.16
  251.3 41.1 all-gather.8
  294.2 36.3 all-gather.12
Sparse Core Ops, SparseCore 1:
  22.2 180.0 reduce-scatter.1
where the time goes:
time: 344 us; the launch traced here: 343 us
  waiting for transfers between devices  224 us (65%)
  blocking collectives  71.1 us (21%)
  matrix products  29.9 us (9%)
  between operations  15 us (4%)
    all_gather x1, waiting for transfers between devices, shards(): lax.all_gather(a_high, 'rep', axis=0, tiled=True)  77.2 us
    psum x1, blocking collectives, shards(): lax.psum((partial_value[0], partial_value[1], partial_value[2]), 'tp')  71.1 us
    all_gather x1, waiting for transfers between devices, shards(): lax.all_gather(a_mid, 'rep', axis=0, tiled=True)  67.6 us
    all_gather x1, waiting for transfers between devices, shards(): lax.all_gather(a_low, 'rep', axis=0, tiled=True)  40.2 us
    all_gather x1, waiting for transfers between devices, shards(): lax.all_gather(b_mid, 'rep', axis=0, tiled=True)  34 us
    dot_general x3, matrix products, shards(): jnp.dot(spread, pieces[b].reshape(count * rank, cols), preferred_element_...  11.2 us
    dot_general x1, matrix products, shards(): base_terms = jnp.dot(acts, base_weight, preferred_element_type=jnp.float32)  9.75 us
    dot_general x3, matrix products, shrink_part(): jnp.einsum('rd,kd->rk', inputs, piece.reshape(count * rank, width), prefe...  8.95 us
  transfers between devices with their start and end apart: 7, of which 5 were waited for; matrix products, arithmetic and copies ran while one was open for 8% of the time, Pallas kernels for 0%

commit v1 on v0

v1 whole, which is shorter than its diff:
```python
import functools

import jax
import jax.numpy as jnp
from jax import lax
from jax.experimental import pallas as pl
from jax.experimental.pallas import tpu as pltpu
from jax.sharding import PartitionSpec as P

F32 = jnp.float32
BF16 = jnp.bfloat16
MESH = pl.DeviceIdType.MESH
ROWS = 384
HALF = 192
COLS = 512
PART = 256
RANKS = 448
PAIR = 2 * RANKS
LANES = 128
OPP, NEXT, PREV, OWN = range(4)
STEP = (2, 1, 3, 0)
TILES = ((OPP, 0), (OPP, 1), (NEXT, 1), (PREV, 0), (NEXT, 0), (PREV, 1), (OWN, 0), (OWN, 1))
AHEAD = 2


def dot(a, b):
    return jnp.dot(a, b, preferred_element_type=F32)


def dot_nt(a, b):
    return lax.dot_general(a, b, (((1,), (1,)), ((), ())), preferred_element_type=F32)


def pair_codes(pair):
    lane = lax.broadcasted_iota(jnp.int32, (1, LANES), 1).astype(F32)
    mid = jnp.floor(lane * (1.0 / 32.0))
    low = jnp.floor(lane * (1.0 / 8.0))
    none = jnp.zeros_like(lane)
    return (
        none + 4.0 * pair,
        none + (4.0 * pair + 1.0),
        mid + (16.0 + 8.0 * pair),
        low + (48.0 + 16.0 * pair),
        none + (4.0 * pair + 2.0),
        none + (4.0 * pair + 3.0),
        mid + (20.0 + 8.0 * pair),
    )


def kernel(
    acts,
    weight,
    a_high,
    a_mid,
    a_low,
    b_high,
    b_mid,
    b_low,
    ids,
    home_high,
    home_mid,
    home_low,
    out,
    xs,
    wb,
    a_all,
    b_all,
    ids_all,
    codes,
    m_send,
    m_recv,
    z_send,
    z_recv,
    own_sum,
    shr,
    shr_y,
    shr_z,
    shr_sum,
    shr_b,
    delta,
    delta_send,
    delta_recv,
    spread,
    local_sems,
    send_sems,
    recv_sems,
):
    rep = lax.axis_index("rep")
    tp = lax.axis_index("tp")
    x, z_lo, core = rep // 4, lax.rem(rep // 2, 2), lax.rem(rep, 2)
    y, z_hi = tp // 4, lax.rem(tp, 4)

    def peer(dx=0, dy=0, dz=0, flip_z=0, flip_core=0):
        to_rep = (
            lax.rem(x + dx, 4) * 4
            + lax.rem(z_lo + flip_z, 2) * 2
            + lax.rem(core + flip_core, 2)
        )
        return (to_rep, lax.rem(y + dy, 4) * 4 + lax.rem(z_hi + dz, 4))

    y_next, y_prev, y_opp = peer(dy=1), peer(dy=3), peer(dy=2)
    z_next, z_prev, z_opp = peer(dz=1), peer(dz=3), peer(dz=2)
    x_next, x_prev = peer(dx=1), peer(dx=3)
    mate, other = peer(flip_core=1), peer(flip_z=1)
    peers = (y_next, y_prev, y_opp, z_next, z_prev, z_opp, x_next, x_prev, mate, other)

    n_local = [0]

    def fetch(src, dst):
        copy = pltpu.make_async_copy(src, dst, local_sems.at[n_local[0]])
        n_local[0] += 1
        copy.start()
        return copy

    sent = []

    def send(src, dst, to):
        copy = pltpu.make_async_remote_copy(
            src_ref=src,
            dst_ref=dst,
            send_sem=send_sems.at[len(sent)],
            recv_sem=recv_sems.at[len(sent)],
            device_id=to,
            device_id_type=MESH,
        )
        copy.start()
        sent.append(copy)
        return copy

    barrier = pltpu.get_barrier_semaphore()
    for to in peers:
        pl.semaphore_signal(barrier, inc=1, device_id=to, device_id_type=MESH)

    got_x = fetch(acts, xs.at[pl.ds(0, ROWS)])

    def fetch_weight(group, place):
        block = lax.rem(y + STEP[place], 4) * 4 + lax.rem(z_hi + STEP[group], 4)
        start = pl.multiple_of(block * COLS, COLS)
        return fetch(weight.at[:, pl.ds(start, COLS)], wb.at[group, place])

    got_w = {}
    for place in range(4):
        got_w[OPP, place] = fetch_weight(OPP, place)
    got_a = (
        fetch(a_high, a_all.at[0, pl.ds(0, 256)]),
        fetch(a_mid, a_all.at[0, pl.ds(256, 128)]),
        fetch(a_low, a_all.at[0, pl.ds(384, 64)]),
    )
    got_ids = fetch(ids, ids_all.at[0])
    for group in (NEXT, PREV, OWN):
        for place in range(4):
            got_w[group, place] = fetch_weight(group, place)
    got_b = (
        fetch(b_high, b_all.at[0, pl.ds(0, 256)]),
        fetch(b_mid, b_all.at[0, pl.ds(256, 128)]),
        fetch(b_low, b_all.at[0, pl.ds(384, 64)]),
    )

    def rows_of(t):
        return xs[pl.ds(TILES[t][1] * HALF, HALF), :]

    def w_of(t, place):
        return wb.at[TILES[t][0], place]

    LEFT, RIGHT = pl.ds(0, PART), pl.ds(PART, PART)
    arrive = {}

    def first(t):
        if (TILES[t][0], OPP) in got_w:
            for place in range(4):
                got_w.pop((TILES[t][0], place)).wait()
        rows = rows_of(t)
        far = dot(rows, w_of(t, OPP)[...]).astype(BF16)
        m_send[t, 0] = far[:, :PART]
        m_send[t, 1] = far[:, PART:]
        m_send[t, 2] = dot(rows, w_of(t, NEXT)[:, RIGHT]).astype(BF16)
        m_send[t, 3] = dot(rows, w_of(t, PREV)[:, LEFT]).astype(BF16)

    def first_send(t):
        for k, to in ((0, y_next), (1, y_prev), (2, y_next), (3, y_prev)):
            arrive[t, k] = send(m_send.at[t, k], m_recv.at[t, k], to)

    def second(t):
        rows = rows_of(t)
        arrive[t, 0].wait_recv()
        near = dot(rows, w_of(t, NEXT)[:, LEFT])
        m_send[t, 4] = (near + m_recv[t, 0].astype(F32)).astype(BF16)
        arrive[t, 4] = send(m_send.at[t, 4], m_recv.at[t, 4], y_next)
        arrive[t, 1].wait_recv()
        near = dot(rows, w_of(t, PREV)[:, RIGHT])
        m_send[t, 5] = (near + m_recv[t, 1].astype(F32)).astype(BF16)
        arrive[t, 5] = send(m_send.at[t, 5], m_recv.at[t, 5], y_prev)

    z_arrive = {}
    Z_PLACE = (z_next, z_prev, z_next, z_prev, z_next, z_prev)

    def third(t):
        group, half = TILES[t]
        own = dot(rows_of(t), w_of(t, OWN)[...])
        for k in (2, 3, 4, 5):
            arrive[t, k].wait_recv()
        left = own[:, :PART] + (m_recv[t, 4].astype(F32) + m_recv[t, 3].astype(F32))
        right = own[:, PART:] + (m_recv[t, 5].astype(F32) + m_recv[t, 2].astype(F32))
        if t in (4, 5):
            z_arrive[t - 4].wait_recv()
            left = left + z_recv[t - 4, :, LEFT].astype(F32)
            right = right + z_recv[t - 4, :, RIGHT].astype(F32)
        if group == OWN:
            own_sum[pl.ds(half * HALF, HALF), LEFT] = left
            own_sum[pl.ds(half * HALF, HALF), RIGHT] = right
        else:
            z_send[t, :, LEFT] = left.astype(BF16)
            z_send[t, :, RIGHT] = right.astype(BF16)
            z_arrive[t] = send(z_send.at[t], z_recv.at[t], Z_PLACE[t])

    def spread_own(store, landed):
        landed["next"] = send(store.at[0, pl.ds(0, RANKS)], store.at[PREV, pl.ds(0, RANKS)], x_next)
        landed["prev"] = send(store.at[0, pl.ds(0, RANKS)], store.at[NEXT, pl.ds(0, RANKS)], x_prev)

    def to_mate(store, landed, pair):
        landed[pair] = (
            send(store.at[pair, pl.ds(0, 384)], store.at[pair, pl.ds(512, 384)], mate),
            send(store.at[pair, pl.ds(384, 64)], store.at[pair, pl.ds(448, 64)], mate),
        )

    def forward(store, landed):
        half = RANKS // 2
        landed["next"].wait_recv()
        landed["far_next"] = send(
            store.at[PREV, pl.ds(0, half)], store.at[3, pl.ds(0, half)], x_next
        )
        landed["prev"].wait_recv()
        landed["far_prev"] = send(
            store.at[NEXT, pl.ds(half, half)], store.at[3, pl.ds(half, half)], x_prev
        )
        to_mate(store, landed, PREV)
        to_mate(store, landed, NEXT)

    def forward_far(store, landed):
        landed["far_next"].wait_recv()
        landed["far_prev"].wait_recv()
        to_mate(store, landed, 3)

    def wait_pair(landed, pair):
        for copy in landed[pair]:
            copy.wait_recv()

    def number_rows():
        def place(owner):
            owner_x = owner // 4
            away = lax.rem(owner_x - x + 4, 4)
            slot = jnp.where(away == 0, 0, jnp.where(away == 1, NEXT, jnp.where(away == 3, PREV, 3)))
            same = lax.rem(owner // 2, 2) == z_lo
            return same, slot * 2 + lax.rem(lax.rem(owner, 2) + core, 2)

        def numbers(home, each, base):
            store = home[...]
            same, slot = place(store // each)
            return jnp.where(same, base + slot * each + lax.rem(store, each) + 1, 0).astype(F32)

        tables = (
            numbers(home_high, 2, 0),
            numbers(home_mid, 4, 16),
            numbers(home_low, 8, 48),
        )
        offsets = (0.0, 32.0, 96.0)
        eye = lax.broadcasted_iota(jnp.int32, (LANES, LANES), 0) == lax.broadcasted_iota(
            jnp.int32, (LANES, LANES), 1
        )
        for part in range(2):
            for block in range(3):
                row_ids = ids_all[part, pl.ds(block, 1), :].astype(F32)
                column = jnp.sum(jnp.where(eye, row_ids, 0.0), axis=1, keepdims=True)
                found = jnp.zeros((LANES, 1), F32)
                for table, offset in zip(tables, offsets):
                    lane = lax.broadcasted_iota(jnp.int32, (1, table.shape[1]), 1).astype(F32)
                    hit = column == lane + offset
                    found = found + jnp.sum(jnp.where(hit, table, 0.0), axis=1, keepdims=True)
                start = part * ROWS + block * LANES
                codes[pl.ds(start, LANES), :] = jnp.broadcast_to(found - 1.0, (LANES, LANES))

    def shrink(pair):
        wait_pair(landed_a, pair)
        tiles = pair_codes(pair)

        @pl.loop(0, 2)
        def _(part):
            rows = pl.ds(pl.multiple_of(part * ROWS, ROWS), ROWS)
            products = dot_nt(xs[rows, :], a_all[pair])
            code = codes[rows, :]
            total = jnp.zeros((ROWS, LANES), F32) if pair == 0 else shr[rows, :]
            for k, tile in enumerate(tiles):
                total = total + jnp.where(code == tile, products[:, k * LANES : (k + 1) * LANES], 0.0)
            shr[rows, :] = total

    SHR_Y, SHR_Z = 192, 48

    def shrink_y():
        for k, (step, to) in enumerate(((1, y_next), (3, y_prev), (2, y_opp))):
            start = pl.multiple_of(lax.rem(y + step, 4) * SHR_Y, SHR_Y)
            z_arrive["y", k] = send(shr.at[pl.ds(start, SHR_Y)], shr_y.at[k], to)

    def shrink_z():
        for k in range(3):
            z_arrive["y", k].wait_recv()
        start = pl.multiple_of(y * SHR_Y, SHR_Y)
        shr_sum[...] = (shr[pl.ds(start, SHR_Y), :] + shr_y[0]) + (shr_y[1] + shr_y[2])
        for k, (step, to) in enumerate(((1, z_next), (3, z_prev), (2, z_opp))):
            start = pl.multiple_of(lax.rem(z_hi + step, 4) * SHR_Z, SHR_Z)
            z_arrive["z", k] = send(shr_sum.at[pl.ds(start, SHR_Z)], shr_z.at[k], to)

    def gather_z():
        for k in range(3):
            z_arrive["z", k].wait_recv()
        start = pl.multiple_of(z_hi * SHR_Z, SHR_Z)
        total = (shr_sum[pl.ds(start, SHR_Z), :] + shr_z[0]) + (shr_z[1] + shr_z[2])
        mine = pl.ds(pl.multiple_of(y * SHR_Y + z_hi * SHR_Z, SHR_Z), SHR_Z)
        shr_b[mine, :] = total.astype(BF16)
        for k, to in enumerate((z_next, z_prev, z_opp)):
            z_arrive["gz", k] = send(shr_b.at[mine], shr_b.at[mine], to)

    def gather_y():
        for k in range(3):
            z_arrive["gz", k].wait_recv()
        mine = pl.ds(pl.multiple_of(y * SHR_Y, SHR_Y), SHR_Y)
        for k, to in enumerate((y_next, y_prev, y_opp)):
            z_arrive["gy", k] = send(shr_b.at[mine], shr_b.at[mine], to)

    def spread_rows(part):
        if part == 1:
            for k in range(3):
                z_arrive["gy", k].wait_recv()
        rows = pl.ds(part * ROWS, ROWS)
        code = codes[rows, :]
        value = shr_b[rows, :].astype(F32)
        for pair in range(4):
            for k, tile in enumerate(pair_codes(pair)):
                lanes = pl.ds(pair * PAIR + k * LANES, LANES)
                spread[:, lanes] = jnp.where(code == tile, value, 0.0).astype(BF16)

    def expand(part):
        spread_rows(part)
        total = dot(spread[...], b_all[...].reshape(4 * PAIR, COLS))
        if part == 1:
            delta_send[...] = total.astype(BF16)
            z_arrive["delta"] = send(delta_send, delta_recv, other)
        else:
            delta[...] = total

    def finish():
        z_arrive["delta"].wait_recv()
        for half in range(2):
            rows = pl.ds(half * HALF, HALF)
            near, far = (4, 3) if half == 0 else (5, 2)
            z_arrive[near].wait_recv()
            z_arrive[far].wait_recv()
            base = own_sum[rows, :] + (z_recv[near].astype(F32) + z_recv[far].astype(F32))
            out[rows, :] = (base + (delta[rows, :] + delta_recv[rows, :].astype(F32))).astype(BF16)

    landed_a, landed_b = {}, {}
    got_x.wait()
    first(0)
    pl.semaphore_wait(barrier, len(peers))
    first_send(0)
    for copy in got_a:
        copy.wait()
    spread_own(a_all, landed_a)
    to_mate(a_all, landed_a, 0)
    x_other = send(xs.at[pl.ds(0, ROWS)], xs.at[pl.ds(ROWS, ROWS)], other)
    got_ids.wait()
    ids_other = send(ids_all.at[0], ids_all.at[1], other)
    first(1)
    first_send(1)
    second(0)
    first(2)
    first_send(2)
    second(1)
    third(0)
    forward(a_all, landed_a)
    ids_other.wait_recv()
    number_rows()
    first(3)
    first_send(3)
    second(2)
    third(1)
    x_other.wait_recv()
    shrink(0)
    for copy in got_b:
        copy.wait()
    spread_own(b_all, landed_b)
    to_mate(b_all, landed_b, 0)
    forward_far(a_all, landed_a)
    shrink(NEXT)
    first(4)
    first_send(4)
    second(3)
    shrink(PREV)
    third(2)
    shrink(3)
    shrink_y()
    first(5)
    first_send(5)
    second(4)
    third(3)
    shrink_z()
    forward(b_all, landed_b)
    first(6)
    first_send(6)
    second(5)
    gather_z()
    third(4)
    first(7)
    first_send(7)
    gather_y()
    second(6)
    forward_far(b_all, landed_b)
    third(5)
    second(7)
    for pair in (0, NEXT, PREV, 3):
        wait_pair(landed_b, pair)
    expand(1)
    expand(0)
    third(6)
    third(7)
    finish()
    for copy in sent:
        copy.wait_send()


N_LOCAL = 24
N_REMOTE = 100


def shards(
    acts,
    base_weight,
    a_high,
    b_high,
    a_mid,
    b_mid,
    a_low,
    b_low,
    row_adapter,
    home_high,
    home_mid,
    home_low,
):
    anywhere = pl.BlockSpec(memory_space=pl.ANY)
    vmem = pl.BlockSpec(memory_space=pltpu.VMEM)
    return pl.pallas_call(
        kernel,
        out_shape=jax.ShapeDtypeStruct((ROWS, COLS), BF16),
        in_specs=[anywhere] * 9 + [vmem] * 3,
        out_specs=vmem,
        scratch_shapes=[
            pltpu.VMEM((2 * ROWS, COLS), BF16),
            pltpu.VMEM((4, 4, COLS, COLS), BF16),
            pltpu.VMEM((4, PAIR, COLS), BF16),
            pltpu.VMEM((4, PAIR, COLS), BF16),
            pltpu.VMEM((2, 3, LANES), jnp.int32),
            pltpu.VMEM((2 * ROWS, LANES), F32),
            pltpu.VMEM((8, 6, HALF, PART), BF16),
            pltpu.VMEM((8, 6, HALF, PART), BF16),
            pltpu.VMEM((6, HALF, COLS), BF16),
            pltpu.VMEM((6, HALF, COLS), BF16),
            pltpu.VMEM((ROWS, COLS), F32),
            pltpu.VMEM((2 * ROWS, LANES), F32),
            pltpu.VMEM((3, 192, LANES), F32),
            pltpu.VMEM((3, 48, LANES), F32),
            pltpu.VMEM((192, LANES), F32),
            pltpu.VMEM((2 * ROWS, LANES), BF16),
            pltpu.VMEM((ROWS, COLS), F32),
            pltpu.VMEM((ROWS, COLS), BF16),
            pltpu.VMEM((ROWS, COLS), BF16),
            pltpu.VMEM((ROWS, 4 * PAIR), BF16),
            pltpu.SemaphoreType.DMA((N_LOCAL,)),
            pltpu.SemaphoreType.DMA((N_REMOTE,)),
            pltpu.SemaphoreType.DMA((N_REMOTE,)),
        ],
        compiler_params=pltpu.CompilerParams(
            collective_id=0, has_side_effects=True, vmem_limit_bytes=58 * 2**20
        ),
        cost_estimate=pl.CostEstimate(
            flops=9_000_000_000, bytes_accessed=16_000_000, transcendentals=0
        ),
        name="project",
    )(
        acts,
        base_weight,
        a_high.reshape(256, COLS),
        a_mid.reshape(128, COLS),
        a_low.reshape(64, COLS),
        b_high.reshape(256, COLS),
        b_mid.reshape(128, COLS),
        b_low.reshape(64, COLS),
        row_adapter.reshape(3, LANES),
        home_high.reshape(1, 32),
        home_mid.reshape(1, 64),
        home_low.reshape(1, 128),
    )


def solution(mesh):
    return jax.shard_map(
        shards,
        mesh=mesh,
        in_specs=(
            P("rep", "tp"),
            P("tp", None),
            P("rep", None, "tp"),
            P("rep", None, "tp"),
            P("rep", None, "tp"),
            P("rep", None, "tp"),
            P("rep", None, "tp"),
            P("rep", None, "tp"),
            P("rep"),
            P(),
            P(),
            P(),
        ),
        out_specs=P("rep", "tp"),
        check_vma=False,
    )
```

time: 344 us -> 80.9 us (0.24)
  waiting for transfers between devices: 224 us -> 0 us
  Pallas kernels: 0 us -> 78.1 us
  blocking collectives: 71.1 us -> 0 us
  matrix products: 29.9 us -> 0 us
  between operations: 15 us -> 0.01 us
    all_gather x6 -> x0, waiting for transfers between devices: 221 us -> none  [the longest x1 77.2 us: shards(): lax.all_gather(a_high, 'rep', axis=0, tiled=True)]
    pallas_call x0 -> x1, Pallas kernels: none -> 78.1 us  [shards(): pl.pallas_call(kernel, out_shape=jax.ShapeDtypeStruct((ROWS, COLS), BF16)...]
    psum x1 -> x0, blocking collectives: 71.1 us -> none  [shards(): lax.psum((partial_value[0], partial_value[1], partial_value[2]), 'tp')]
    dot_general x7 -> x0, matrix products: 29.9 us -> none  [the longest x3 11.2 us: shards(): jnp.dot(spread, pieces[b].reshape(count * rank, cols), preferred_element_...]
  transfers between devices with their start and end apart: 7 -> 0, of which waited for: 5 -> 0; matrix products, arithmetic and copies ran while one was open for 8% -> 0% of each run, Pallas kernels for 0% -> 0%
where the time goes in v1:
time: 80.9 us; the launch traced here: 79.8 us
  Pallas kernels  78.1 us (97%)
  local copies, waits for them, and re-layouts  1.77 us (2%)
    pallas_call x1, Pallas kernels, shards(): pl.pallas_call(kernel, out_shape=jax.ShapeDtypeStruct((ROWS, COLS), BF16)...  78.1 us
    unnamed x1, local copies, waits for them, and re-layouts  1.77 us

profile of v1, /device:TPU:1, one launch (start us, length us, event | category | flops | bytes accessed | tf_op | source)
XLA Modules:
  0.0 79.8 jit_solution(9436354038424534333)
XLA Ops:
  0.0 78.1 %project.1 = bf16[384,512]{1,0:T(8,128)(2,1)} custom-call(bf16[384,512]{1,0:T(8,128)(2,1)} %acts.1, bf16[512,8192]{1,0:T(8,128)(2,1)} %weight.1, bf16[256,512]{1,0:T(8,128)(2,1)} %bitcast.10, bf16[128,512]{1,0:T(8,128)(2,1)} %bitcast.12, bf16[64,512]{1,0:T(8,128)(2,1)} %bitcast.14, bf16[256,512]{1,0:T(8,128)(2,1)} %bitcast.11, bf16[128,512]{1,0:T(8,128)(2,1)} %bitcast.13, ...), custom_call_target="tpu_custom_call" | custom-call | flops 8999999488 | bytes 16000000 | tf_op jit(solution)/shard_map/project/pallas_call | solution.py:450
  78.1 1.8 %copy.14 = bf16[384,512]{1,0:T(8,128)(2,1)} copy(bf16[384,512]{1,0:T(8,128)(2,1)} %project.1) | data formatting | bytes 786432

commit v2 on v1

v2 whole, which is shorter than its diff:
```python
import functools

import jax
import jax.numpy as jnp
from jax import lax
from jax.experimental import pallas as pl
from jax.experimental.pallas import tpu as pltpu
from jax.sharding import PartitionSpec as P

F32 = jnp.float32
BF16 = jnp.bfloat16
MESH = pl.DeviceIdType.MESH
ROWS = 384
TALL = 96
SHR_Y, SHR_Z = 96, 24
PIECE = 224
COLS = 512
PART = 256
RANKS = 448
PAIR = 2 * RANKS
LANES = 128
OPP, NEXT, PREV, OWN = range(4)
STEP = (2, 1, 3, 0)
TILES = (
    ((OPP, 0), (OPP, 2), (OPP, 1), (OPP, 3))
    + ((NEXT, 2), (PREV, 0), (NEXT, 3), (PREV, 1))
    + ((NEXT, 0), (PREV, 2), (NEXT, 1), (PREV, 3))
    + ((OWN, 0), (OWN, 2), (OWN, 1), (OWN, 3))
)
TO_NEXT = {(OPP, 0), (OPP, 1), (NEXT, 0), (NEXT, 1), (NEXT, 2), (NEXT, 3)}


def dot(a, b):
    return jnp.dot(a, b, preferred_element_type=F32)


def dot_nt(a, b):
    return lax.dot_general(a, b, (((1,), (1,)), ((), ())), preferred_element_type=F32)


def pair_codes(pair):
    lane = lax.broadcasted_iota(jnp.int32, (1, LANES), 1).astype(F32)
    mid = jnp.floor(lane * (1.0 / 32.0))
    low = jnp.floor(lane * (1.0 / 8.0))
    none = jnp.zeros_like(lane)
    return (
        none + 4.0 * pair,
        none + (4.0 * pair + 1.0),
        mid + (16.0 + 8.0 * pair),
        low + (48.0 + 16.0 * pair),
        none + (4.0 * pair + 2.0),
        none + (4.0 * pair + 3.0),
        mid + (20.0 + 8.0 * pair),
    )


def kernel(
    acts,
    weight,
    a_high,
    a_mid,
    a_low,
    b_high,
    b_mid,
    b_low,
    ids,
    home_high,
    home_mid,
    home_low,
    out,
    xs,
    wb,
    a_all,
    b_all,
    ids_all,
    codes,
    codes_other,
    m_send,
    m_recv,
    z_send,
    z_recv,
    own_sum,
    shr,
    shr_part,
    shr_y,
    shr_z,
    shr_sum,
    shr_round,
    shr_b,
    delta,
    local_sems,
    send_sems,
    recv_sems,
):
    rep = lax.axis_index("rep")
    tp = lax.axis_index("tp")
    x, z_lo, core = rep // 4, lax.rem(rep // 2, 2), lax.rem(rep, 2)
    y, z_hi = tp // 4, lax.rem(tp, 4)

    def peer(dx=0, dy=0, dz=0, flip_z=0, flip_core=0):
        to_rep = (
            lax.rem(x + dx, 4) * 4
            + lax.rem(z_lo + flip_z, 2) * 2
            + lax.rem(core + flip_core, 2)
        )
        return (to_rep, lax.rem(y + dy, 4) * 4 + lax.rem(z_hi + dz, 4))

    y_next, y_prev = peer(dy=1), peer(dy=3)
    z_next, z_prev = peer(dz=1), peer(dz=3)
    x_next, x_prev = peer(dx=1), peer(dx=3)
    mate, other = peer(flip_core=1), peer(flip_z=1)
    y_opp, z_opp = peer(dy=2), peer(dz=2)
    peers = (y_next, y_prev, y_opp, z_next, z_prev, z_opp, x_next, x_prev, mate, other)

    n_local = [0]

    def fetch(src, dst):
        copy = pltpu.make_async_copy(src, dst, local_sems.at[n_local[0]])
        n_local[0] += 1
        copy.start()
        return copy

    sent = []

    def send(src, dst, to):
        copy = pltpu.make_async_remote_copy(
            src_ref=src,
            dst_ref=dst,
            send_sem=send_sems.at[len(sent)],
            recv_sem=recv_sems.at[len(sent)],
            device_id=to,
            device_id_type=MESH,
        )
        copy.start()
        sent.append(copy)
        return copy

    barrier = pltpu.get_barrier_semaphore()
    for to in peers:
        pl.semaphore_signal(barrier, inc=1, device_id=to, device_id_type=MESH)

    got_x = fetch(acts, xs.at[pl.ds(0, ROWS)])

    def fetch_weight(group, place):
        block = lax.rem(y + STEP[place], 4) * 4 + lax.rem(z_hi + STEP[group], 4)
        start = pl.multiple_of(block * COLS, COLS)
        return fetch(weight.at[:, pl.ds(start, COLS)], wb.at[group, place])

    got_w = {}
    for place in range(4):
        got_w[OPP, place] = fetch_weight(OPP, place)
    got_a = (
        fetch(a_high, a_all.at[0, pl.ds(0, 256)]),
        fetch(a_mid, a_all.at[0, pl.ds(256, 128)]),
        fetch(a_low, a_all.at[0, pl.ds(384, 64)]),
    )
    got_ids = fetch(ids, ids_all.at[0])
    for group in (NEXT, PREV, OWN):
        for place in range(4):
            got_w[group, place] = fetch_weight(group, place)
    got_b = (
        fetch(b_high, b_all.at[0, pl.ds(0, 256)]),
        fetch(b_mid, b_all.at[0, pl.ds(256, 128)]),
        fetch(b_low, b_all.at[0, pl.ds(384, 64)]),
    )

    def rows_of(t):
        return xs[pl.ds(TILES[t][1] * TALL, TALL), :]

    def w_of(t, place):
        return wb.at[TILES[t][0], place]

    LEFT, RIGHT = pl.ds(0, PART), pl.ds(PART, PART)
    arrive = {}

    def across(t, k):
        to = y_next if k % 2 == 0 else y_prev
        arrive[t, k] = send(m_send.at[t, k], m_recv.at[t, k], to)

    def first(t):
        if (TILES[t][0], OPP) in got_w:
            for place in range(4):
                got_w.pop((TILES[t][0], place)).wait()
        far = dot(rows_of(t), w_of(t, OPP)[...]).astype(BF16)
        m_send[t, 0] = far[:, :PART]
        m_send[t, 1] = far[:, PART:]

    def first_send(t):
        across(t, 0)
        across(t, 1)

    def direct(t):
        rows = rows_of(t)
        m_send[t, 2] = dot(rows, w_of(t, NEXT)[:, RIGHT]).astype(BF16)
        across(t, 2)
        m_send[t, 3] = dot(rows, w_of(t, PREV)[:, LEFT]).astype(BF16)
        across(t, 3)

    def second(t):
        rows = rows_of(t)
        for k, place, cols in ((0, NEXT, LEFT), (1, PREV, RIGHT)):
            arrive[t, k].wait_recv()
            near = dot(rows, w_of(t, place)[:, cols])
            m_send[t, k + 4] = (near + m_recv[t, k].astype(F32)).astype(BF16)
            across(t, k + 4)

    z_arrive = {}

    def third(t):
        group, quarter = TILES[t]
        own = dot(rows_of(t), w_of(t, OWN)[...])
        for k in (2, 3, 4, 5):
            arrive[t, k].wait_recv()
        left = own[:, :PART] + (m_recv[t, 4].astype(F32) + m_recv[t, 3].astype(F32))
        right = own[:, PART:] + (m_recv[t, 5].astype(F32) + m_recv[t, 2].astype(F32))
        if 8 <= t < 12:
            z_arrive[t - 8].wait_recv()
            left = left + z_recv[t - 8, :, LEFT].astype(F32)
            right = right + z_recv[t - 8, :, RIGHT].astype(F32)
        if group == OWN:
            own_sum[pl.ds(quarter * TALL, TALL), LEFT] = left
            own_sum[pl.ds(quarter * TALL, TALL), RIGHT] = right
        else:
            z_send[t, :, LEFT] = left.astype(BF16)
            z_send[t, :, RIGHT] = right.astype(BF16)
            to = z_next if TILES[t] in TO_NEXT else z_prev
            z_arrive[t] = send(z_send.at[t], z_recv.at[t], to)

    def spread_own(store, landed, n, base=0):
        low, high = pl.ds(0, PIECE), pl.ds(PIECE, PIECE)
        ahead, behind = (low, high) if n == 0 else (high, low)
        landed["next", n] = send(store.at[base, ahead], store.at[base + PREV, ahead], x_next)
        landed["prev", n] = send(store.at[base, behind], store.at[base + NEXT, behind], x_prev)

    def to_mate(store, landed, pair, base=0):
        block = base + pair
        landed[pair] = (
            send(store.at[block, pl.ds(0, 384)], store.at[block, pl.ds(512, 384)], mate),
            send(store.at[block, pl.ds(384, 64)], store.at[block, pl.ds(448, 64)], mate),
        )

    def forward(store, landed, base=0):
        low, high = pl.ds(0, PIECE), pl.ds(PIECE, PIECE)
        landed["next", 0].wait_recv()
        landed["far_next"] = send(store.at[base + PREV, low], store.at[base + 3, low], x_next)
        landed["prev", 0].wait_recv()
        landed["far_prev"] = send(store.at[base + NEXT, high], store.at[base + 3, high], x_prev)

    def forward_near(store, landed, base=0):
        landed["next", 1].wait_recv()
        to_mate(store, landed, PREV, base)
        landed["prev", 1].wait_recv()
        to_mate(store, landed, NEXT, base)

    def forward_far(store, landed, base=0):
        landed["far_next"].wait_recv()
        landed["far_prev"].wait_recv()
        to_mate(store, landed, 3, base)

    def wait_pair(landed, pair):
        for copy in landed[pair]:
            copy.wait_recv()

    def number_rows():
        def place(owner):
            owner_x = owner // 4
            away = lax.rem(owner_x - x + 4, 4)
            slot = jnp.where(away == 0, 0, jnp.where(away == 1, NEXT, jnp.where(away == 3, PREV, 3)))
            same = lax.rem(owner // 2, 2) == z_lo
            return same.astype(jnp.int32), slot * 2 + lax.rem(lax.rem(owner, 2) + core, 2)

        def numbers(home, each, base):
            store = home[...]
            same, slot = place(store // each)
            number = base + slot * each + lax.rem(store, each) + 1
            return tuple(jnp.where(same == k, number, 0).astype(F32) for k in (1, 0))

        tables = (
            numbers(home_high, 2, 0),
            numbers(home_mid, 4, 16),
            numbers(home_low, 8, 48),
        )
        offsets = (0.0, 32.0, 96.0)
        eye = lax.broadcasted_iota(jnp.int32, (LANES, LANES), 0) == lax.broadcasted_iota(
            jnp.int32, (LANES, LANES), 1
        )
        for part in range(2):
            for block in range(3):
                row_ids = ids_all[part, pl.ds(block, 1), :].astype(F32)
                column = jnp.sum(jnp.where(eye, row_ids, 0.0), axis=1, keepdims=True)
                start = part * ROWS + block * LANES
                for side, store in ((0, codes), (1, codes_other))[: 2 - part]:
                    found = jnp.zeros((LANES, 1), F32)
                    for table, offset in zip(tables, offsets):
                        lane = lax.broadcasted_iota(jnp.int32, (1, table[side].shape[1]), 1)
                        hit = column == lane.astype(F32) + offset
                        found = found + jnp.sum(
                            jnp.where(hit, table[side], 0.0), axis=1, keepdims=True
                        )
                    store[pl.ds(start, LANES), :] = jnp.broadcast_to(found - 1.0, (LANES, LANES))

    def shrink(pair):
        wait_pair(landed_a, pair)
        tiles = pair_codes(pair)

        @pl.loop(0, 2)
        def _(part):
            rows = pl.ds(pl.multiple_of(part * ROWS, ROWS), ROWS)
            products = dot_nt(xs[rows, :], a_all[pair])
            code = codes[rows, :]
            total = jnp.zeros((ROWS, LANES), F32) if pair == 0 else shr[rows, :]
            for k, tile in enumerate(tiles):
                total = total + jnp.where(code == tile, products[:, k * LANES : (k + 1) * LANES], 0.0)
            shr[rows, :] = total

    AWAY = (1, 3, 2)
    Y_TEAM, Z_TEAM = (y_next, y_prev, y_opp), (z_next, z_prev, z_opp)

    def part_of(index, size):
        return pl.ds(pl.multiple_of(lax.rem(index, 4) * size, size), size)

    def shrink_other():
        z_arrive["other"] = send(shr.at[pl.ds(ROWS, ROWS)], shr_part, other)

    def shrink_y():
        z_arrive["other"].wait_recv()
        shr_part[...] += shr[pl.ds(0, ROWS), :]
        for k in range(3):
            z_arrive["y", k] = send(shr_part.at[part_of(y + AWAY[k], SHR_Y)], shr_y.at[k], Y_TEAM[k])

    def shrink_z():
        for k in range(3):
            z_arrive["y", k].wait_recv()
        shr_sum[...] = (shr_part[part_of(y, SHR_Y), :] + shr_y[0]) + (shr_y[1] + shr_y[2])
        for k in range(3):
            z_arrive["z", k] = send(
                shr_sum.at[part_of(z_hi + AWAY[k], SHR_Z)], shr_z.at[k], Z_TEAM[k]
            )

    def gather_z():
        for k in range(3):
            z_arrive["z", k].wait_recv()
        mine = part_of(z_hi, SHR_Z)
        total = (shr_sum[mine, :] + shr_z[0]) + (shr_z[1] + shr_z[2])
        shr_round[mine, :] = total.astype(BF16).astype(F32)
        for k in range(3):
            z_arrive["gz", k] = send(shr_round.at[mine], shr_round.at[mine], Z_TEAM[k])

    def gather_y():
        for k in range(3):
            z_arrive["gz", k].wait_recv()
        mine = part_of(y, SHR_Y)
        shr_b[mine, :] = shr_round[...].astype(BF16)
        for k in range(3):
            z_arrive["gy", k] = send(shr_b.at[mine], shr_b.at[mine], Y_TEAM[k])

    def wait_shrink():
        for k in range(3):
            z_arrive["gy", k].wait_recv()

    def expand(side):
        landed, code = ((landed_b, codes), (landed_c, codes_other))[side]
        for pair in (0, NEXT, PREV, 3):
            wait_pair(landed, pair)
        code = code[pl.ds(0, ROWS), :].astype(BF16)
        value = shr_b[...]
        none = jnp.zeros_like(value)
        total = delta[...] if side else None
        for pair in range(4):
            tiles = pair_codes(pair)
            piece = jnp.concatenate(
                [jnp.where(code == tile.astype(BF16), value, none) for tile in tiles], axis=1
            )
            part = dot(piece, b_all[side * 4 + pair])
            total = part if total is None else total + part
        delta[...] = total

    def finish():
        for quarter, (near, far) in enumerate(((8, 5), (10, 7), (9, 4), (11, 6))):
            z_arrive[near].wait_recv()
            z_arrive[far].wait_recv()
            rows = pl.ds(quarter * TALL, TALL)
            add = z_recv[near].astype(F32) + z_recv[far].astype(F32)
            out[rows, :] = ((own_sum[rows, :] + add) + delta[rows, :]).astype(BF16)

    landed_a, landed_b, landed_c = {}, {}, {}
    got_x.wait()
    first(0)
    pl.semaphore_wait(barrier, len(peers))
    first_send(0)
    direct(0)
    for copy in got_a:
        copy.wait()
    spread_own(a_all, landed_a, 0)
    spread_own(a_all, landed_a, 1)
    to_mate(a_all, landed_a, 0)
    x_other = send(xs.at[pl.ds(0, ROWS)], xs.at[pl.ds(ROWS, ROWS)], other)
    got_ids.wait()
    ids_other = send(ids_all.at[0], ids_all.at[1], other)
    first(1)
    first_send(1)
    direct(1)
    first(2)
    first_send(2)
    direct(2)
    first(3)
    first_send(3)
    second(0)
    first(4)
    first_send(4)
    direct(3)
    for copy in got_b:
        copy.wait()
    b_other = send(b_all.at[0, pl.ds(0, RANKS)], b_all.at[4, pl.ds(0, RANKS)], other)
    second(1)
    first(5)
    first_send(5)
    direct(4)
    forward(a_all, landed_a)
    spread_own(b_all, landed_b, 0)
    spread_own(b_all, landed_b, 1)
    to_mate(b_all, landed_b, 0)
    second(2)
    first(6)
    first_send(6)
    direct(5)
    second(3)
    first(7)
    first_send(7)
    direct(6)
    second(4)
    first(8)
    first_send(8)
    third(0)
    direct(7)
    forward_near(a_all, landed_a)
    ids_other.wait_recv()
    number_rows()
    x_other.wait_recv()
    second(5)
    first(9)
    first_send(9)
    third(1)
    direct(8)
    shrink(0)
    shrink(1)
    second(6)
    first(10)
    first_send(10)
    third(2)
    direct(9)
    b_other.wait_recv()
    spread_own(b_all, landed_c, 0, 4)
    spread_own(b_all, landed_c, 1, 4)
    to_mate(b_all, landed_c, 0, 4)
    shrink(2)
    forward_far(a_all, landed_a)
    shrink(3)
    shrink_other()
    second(7)
    first(11)
    first_send(11)
    third(3)
    direct(10)
    second(8)
    first(12)
    first_send(12)
    third(4)
    direct(11)
    forward(b_all, landed_b)
    second(9)
    first(13)
    first_send(13)
    third(5)
    direct(12)
    shrink_y()
    forward_near(b_all, landed_b)
    second(10)
    first(14)
    first_send(14)
    third(6)
    direct(13)
    second(11)
    first(15)
    first_send(15)
    third(7)
    direct(14)
    shrink_z()
    forward(b_all, landed_c, 4)
    second(12)
    third(8)
    direct(15)
    gather_z()
    forward_near(b_all, landed_c, 4)
    second(13)
    third(9)
    gather_y()
    forward_far(b_all, landed_b)
    second(14)
    third(10)
    forward_far(b_all, landed_c, 4)
    second(15)
    third(11)
    wait_shrink()
    expand(0)
    expand(1)
    third(12)
    third(13)
    third(14)
    third(15)
    finish()
    for copy in sent:
        copy.wait_send()


N_LOCAL = 24
N_REMOTE = 200


def shards(
    acts,
    base_weight,
    a_high,
    b_high,
    a_mid,
    b_mid,
    a_low,
    b_low,
    row_adapter,
    home_high,
    home_mid,
    home_low,
):
    anywhere = pl.BlockSpec(memory_space=pl.ANY)
    vmem = pl.BlockSpec(memory_space=pltpu.VMEM)
    return pl.pallas_call(
        kernel,
        out_shape=jax.ShapeDtypeStruct((ROWS, COLS), BF16),
        in_specs=[anywhere] * 9 + [vmem] * 3,
        out_specs=vmem,
        scratch_shapes=[
            pltpu.VMEM((2 * ROWS, COLS), BF16),
            pltpu.VMEM((4, 4, COLS, COLS), BF16),
            pltpu.VMEM((4, PAIR, COLS), BF16),
            pltpu.VMEM((8, PAIR, COLS), BF16),
            pltpu.VMEM((2, 3, LANES), jnp.int32),
            pltpu.VMEM((2 * ROWS, LANES), F32),
            pltpu.VMEM((ROWS, LANES), F32),
            pltpu.VMEM((16, 6, TALL, PART), BF16),
            pltpu.VMEM((16, 6, TALL, PART), BF16),
            pltpu.VMEM((12, TALL, COLS), BF16),
            pltpu.VMEM((12, TALL, COLS), BF16),
            pltpu.VMEM((ROWS, COLS), F32),
            pltpu.VMEM((2 * ROWS, LANES), F32),
            pltpu.VMEM((ROWS, LANES), F32),
            pltpu.VMEM((3, SHR_Y, LANES), F32),
            pltpu.VMEM((3, SHR_Z, LANES), F32),
            pltpu.VMEM((SHR_Y, LANES), F32),
            pltpu.VMEM((SHR_Y, LANES), F32),
            pltpu.VMEM((ROWS, LANES), BF16),
            pltpu.VMEM((ROWS, COLS), F32),
            pltpu.SemaphoreType.DMA((N_LOCAL,)),
            pltpu.SemaphoreType.DMA((N_REMOTE,)),
            pltpu.SemaphoreType.DMA((N_REMOTE,)),
        ],
        compiler_params=pltpu.CompilerParams(
            collective_id=0, has_side_effects=True, vmem_limit_bytes=58 * 2**20
        ),
        cost_estimate=pl.CostEstimate(
            flops=9_000_000_000, bytes_accessed=16_000_000, transcendentals=0
        ),
        name="project",
    )(
        acts,
        base_weight,
        a_high.reshape(256, COLS),
        a_mid.reshape(128, COLS),
        a_low.reshape(64, COLS),
        b_high.reshape(256, COLS),
        b_mid.reshape(128, COLS),
        b_low.reshape(64, COLS),
        row_adapter.reshape(3, LANES),
        home_high.reshape(1, 32),
        home_mid.reshape(1, 64),
        home_low.reshape(1, 128),
    )


def solution(mesh):
    return jax.shard_map(
        shards,
        mesh=mesh,
        in_specs=(
            P("rep", "tp"),
            P("tp", None),
            P("rep", None, "tp"),
            P("rep", None, "tp"),
            P("rep", None, "tp"),
            P("rep", None, "tp"),
            P("rep", None, "tp"),
            P("rep", None, "tp"),
            P("rep"),
            P(),
            P(),
            P(),
        ),
        out_specs=P("rep", "tp"),
        check_vma=False,
    )
```

time: 80.9 us -> 78.6 us (0.972); the launches traced: 79.8 us -> 78.5 us
  Pallas kernels: 78.1 us -> 76.7 us
    pallas_call x1, Pallas kernels: 78.1 us -> 76.7 us  [shards(): pl.pallas_call(kernel, out_shape=jax.ShapeDtypeStruct((ROWS, COLS), BF16)...]
where the time goes in v2:
time: 78.6 us; the launch traced here: 78.5 us
  Pallas kernels  76.7 us (98%)
  local copies, waits for them, and re-layouts  1.77 us (2%)
    pallas_call x1, Pallas kernels, shards(): pl.pallas_call(kernel, out_shape=jax.ShapeDtypeStruct((ROWS, COLS), BF16)...  76.7 us
    unnamed x1, local copies, waits for them, and re-layouts  1.77 us

profile of v2, /device:TPU:1, one launch (start us, length us, event | category | flops | bytes accessed | tf_op | source)
XLA Modules:
  0.0 78.5 jit_solution(10583963557553665825)
XLA Ops:
  0.0 76.7 %project.1 = bf16[384,512]{1,0:T(8,128)(2,1)} custom-call(bf16[384,512]{1,0:T(8,128)(2,1)} %acts.1, bf16[512,8192]{1,0:T(8,128)(2,1)} %weight.1, bf16[256,512]{1,0:T(8,128)(2,1)} %bitcast.10, bf16[128,512]{1,0:T(8,128)(2,1)} %bitcast.12, bf16[64,512]{1,0:T(8,128)(2,1)} %bitcast.14, bf16[256,512]{1,0:T(8,128)(2,1)} %bitcast.11, bf16[128,512]{1,0:T(8,128)(2,1)} %bitcast.13, ...), custom_call_target="tpu_custom_call" | custom-call | flops 8999999488 | bytes 16000000 | tf_op jit(solution)/shard_map/project/pallas_call | solution.py:536
  76.7 1.8 %copy.14 = bf16[384,512]{1,0:T(8,128)(2,1)} copy(bf16[384,512]{1,0:T(8,128)(2,1)} %project.1) | data formatting | bytes 786432

commit v3 on v2

--- a/solution.py
+++ b/solution.py
@@ -427,11 +427,12 @@
     second(3)
     first(7)
     first_send(7)
+    third(0)
     direct(6)
     second(4)
     first(8)
     first_send(8)
-    third(0)
+    third(1)
     direct(7)
     forward_near(a_all, landed_a)
     ids_other.wait_recv()
@@ -440,14 +441,14 @@
     second(5)
     first(9)
     first_send(9)
-    third(1)
+    third(2)
     direct(8)
     shrink(0)
     shrink(1)
     second(6)
     first(10)
     first_send(10)
-    third(2)
+    third(3)
     direct(9)
     b_other.wait_recv()
     spread_own(b_all, landed_c, 0, 4)
@@ -460,53 +461,52 @@
     second(7)
     first(11)
     first_send(11)
-    third(3)
+    third(4)
     direct(10)
     second(8)
     first(12)
     first_send(12)
-    third(4)
+    third(5)
     direct(11)
     forward(b_all, landed_b)
     second(9)
     first(13)
     first_send(13)
-    third(5)
+    third(6)
     direct(12)
     shrink_y()
     forward_near(b_all, landed_b)
     second(10)
     first(14)
     first_send(14)
-    third(6)
+    third(7)
     direct(13)
     second(11)
     first(15)
     first_send(15)
-    third(7)
+    third(8)
     direct(14)
     shrink_z()
     forward(b_all, landed_c, 4)
     second(12)
-    third(8)
+    third(9)
     direct(15)
     gather_z()
     forward_near(b_all, landed_c, 4)
     second(13)
-    third(9)
+    third(10)
     gather_y()
     forward_far(b_all, landed_b)
     second(14)
-    third(10)
+    third(11)
     forward_far(b_all, landed_c, 4)
     second(15)
-    third(11)
+    third(12)
+    third(13)
+    third(14)
     wait_shrink()
     expand(0)
     expand(1)
-    third(12)
-    third(13)
-    third(14)
     third(15)
     finish()
     for copy in sent:

time: 78.6 us -> 77.9 us (level); the launches traced: 78.5 us -> 76.4 us
  Pallas kernels: 76.7 us -> 74.6 us
    pallas_call x1, Pallas kernels: 76.7 us -> 74.6 us  [shards(): pl.pallas_call(kernel, out_shape=jax.ShapeDtypeStruct((ROWS, COLS), BF16)...]
where the time goes in v3:
time: 77.9 us; the launch traced here: 76.4 us
  Pallas kernels  74.6 us (96%)
  local copies, waits for them, and re-layouts  1.77 us (2%)
    pallas_call x1, Pallas kernels, shards(): pl.pallas_call(kernel, out_shape=jax.ShapeDtypeStruct((ROWS, COLS), BF16)...  74.6 us
    unnamed x1, local copies, waits for them, and re-layouts  1.77 us

profile of v3, /device:TPU:1, one launch (start us, length us, event | category | flops | bytes accessed | tf_op | source)
XLA Modules:
  0.0 76.4 jit_solution(7794721339851272957)
XLA Ops:
  0.0 74.6 %project.1 = bf16[384,512]{1,0:T(8,128)(2,1)} custom-call(bf16[384,512]{1,0:T(8,128)(2,1)} %acts.1, bf16[512,8192]{1,0:T(8,128)(2,1)} %weight.1, bf16[256,512]{1,0:T(8,128)(2,1)} %bitcast.10, bf16[128,512]{1,0:T(8,128)(2,1)} %bitcast.12, bf16[64,512]{1,0:T(8,128)(2,1)} %bitcast.14, bf16[256,512]{1,0:T(8,128)(2,1)} %bitcast.11, bf16[128,512]{1,0:T(8,128)(2,1)} %bitcast.13, ...), custom_call_target="tpu_custom_call" | custom-call | flops 8999999488 | bytes 16000000 | tf_op jit(solution)/shard_map/project/pallas_call | solution.py:536
  74.6 1.8 %copy.14 = bf16[384,512]{1,0:T(8,128)(2,1)} copy(bf16[384,512]{1,0:T(8,128)(2,1)} %project.1) | data formatting | bytes 786432
